TPU v7x, 512 devices: a whole 4x8x8 slice. The times are simulated.
512 devices in a mesh: ctx: 64 (over z, y), head: 8 (over x, core).
Axes of the slice: x: 4, y: 8, z: 8, core: 2. Of those that a mesh axis runs over, the one named last changes fastest.
Arguments:
- queries: bfloat16 [16384, 4096], P('ctx', 'head'), may hold values from -24 to 24
- keys: bfloat16 [16384, 4096], P('ctx', 'head'), may hold values from -6 to 6
- values: bfloat16 [16384, 4096], P('ctx', 'head'), may hold values from -72 to 72
- out_grad: bfloat16 [16384, 4096], P('ctx', 'head'), may hold values from -6 to 6
- gain: float32 [4096], P('head'), may hold values from 0.1 to 1.9
- segment_ids: int32 [16384], P('ctx'), may hold values from 0 to 7, never falling along the last dimension, each value on 1 to 8192 neighbouring positions
Outputs:
- grad_queries: bfloat16 [16384, 4096], P('ctx', 'head')
- grad_keys: bfloat16 [16384, 4096], P('ctx', 'head')
- grad_values: bfloat16 [16384, 4096], P('ctx', 'head')
Inputs may be any that keep to these rules, and one draw needn't show every extreme that they name: `segment_ids`: ids never fall along the sequence; every document has 1 to 8192 tokens, one exactly that many.
All inputs are finite; a program needn't handle non-finite values.
Results may differ from a plain program's by a relative error of at most 0.0013.
Values sent between devices are 32-bit elements; how exact they have to be, the bound alone decides.
A program may use at most 128 MiB of HBM per device.

v0:
```python
import functools

import jax
import jax.numpy as jnp
from jax import lax
from jax.experimental import pallas as pl
from jax.experimental.pallas import tpu as pltpu
from jax.sharding import PartitionSpec as P

HD = 128
EPSILON = 1e-06
RING = 8
MESH = pl.DeviceIdType.MESH
F32 = jnp.float32
BF16 = jnp.bfloat16


def dot(a, b, ca, cb):
    return lax.dot_general(a, b, (((ca,), (cb,)), ((), ())), preferred_element_type=F32)


def split(x):
    hi = x.astype(BF16)
    return hi, (x - hi.astype(F32)).astype(BF16)


def kernel(
    nctx, nhead, features,
    q_hbm, k_hbm, v_hbm, g_hbm, gain_ref, ids_ref,
    gq_hbm, gk_hbm, gv_hbm,
    q_ref, k_ref, v_ref, g_ref, oq_ref, ok_ref, ov_ref,
    snd, rcv, ps_snd, ps_rcv,
    sc_hi, sc_lo, att, wgt, gr_hi, gr_lo, st_hi, st_lo, lk, lv,
    in_sem, out_sem, send_sem, recv_sem, ps_sem,
):
    rows, width = q_ref.shape
    heads = width // HD
    piece = snd.shape[2] - 8
    nz = nctx // RING
    me = lax.axis_index("ctx")
    z, y = me // RING, me % RING
    h = lax.axis_index("head")

    offsets = [(dz, dy) for dz in range(nz) for dy in range(RING) if dz or dy]
    offsets.sort(key=lambda o: -(min(o[0], nz - o[0]) + min(o[1], RING - o[1])))
    peers = [lax.rem(z + dz, nz) * RING + lax.rem(y + dy, RING) for dz, dy in offsets]

    barrier = pltpu.get_barrier_semaphore()
    for p in peers:
        pl.semaphore_signal(barrier, inc=1, device_id={"ctx": p}, device_id_type=MESH)
    for d in range(1, nhead):
        pl.semaphore_signal(barrier, inc=1, device_id={"head": lax.rem(h + d, nhead)}, device_id_type=MESH)

    loads = [
        pltpu.make_async_copy(src, dst, in_sem.at[i])
        for i, (src, dst) in enumerate(((k_hbm, k_ref), (v_hbm, v_ref), (q_hbm, q_ref), (g_hbm, g_ref)))
    ]
    for copy in loads:
        copy.start()

    def scatter(phase):
        for p in peers:
            pltpu.make_async_remote_copy(
                snd.at[phase, p, pl.ds(0, piece + 1)], rcv.at[phase, me, pl.ds(0, piece + 1)],
                send_sem.at[phase], recv_sem.at[phase],
                device_id={"ctx": p}, device_id_type=MESH,
            ).start()
        rcv[phase, me] = snd[phase, me]

    def gather_wait(phase):
        part = rcv.at[phase, pl.ds(0, nctx - 1), pl.ds(0, piece + 1)]
        pltpu.make_async_copy(part, part, recv_sem.at[phase]).wait()

    def running(phase, backward):
        def step(i, carry):
            total, tag = carry
            e = nctx - 1 - i if backward else i
            snd[phase + 1, e, pl.ds(0, piece)] = total
            snd[phase + 1, e, pl.ds(piece, 1)] = tag
            own = rcv[phase, e, pl.ds(piece, 1)]
            total = rcv[phase, e, pl.ds(0, piece)] + jnp.where(own == tag, total, 0.0)
            return total, own

        lax.fori_loop(0, nctx, step, (jnp.zeros((piece, HD), F32), jnp.full((1, HD), -1.0, F32)), unroll=8)

    def state(phase, i):
        per = HD // piece
        return rcv[phase, pl.ds(i * per, per), pl.ds(0, piece)].reshape(HD, HD)

    def put_state(phase, i, value):
        per = HD // piece
        snd[phase, pl.ds(i * per, per), pl.ds(0, piece)] = value.reshape(per, piece, HD)

    def head(ref, i):
        return ref[:, pl.ds(i * HD, HD)]

    ids = ids_ref[...].astype(F32)
    col = jnp.broadcast_to(ids, (HD, rows)).T
    first, last = ids[:, 0:1], ids[:, rows - 1 : rows]

    snd[0, :, pl.ds(piece, 1)] = jnp.broadcast_to(last[None], (nctx, 1, HD))
    last_mask = (col == last).astype(F32).astype(BF16)
    loads[0].wait()
    loads[1].wait()
    for i in range(heads):
        put_state(0, i, dot(head(k_ref, i) * last_mask, head(v_ref, i), 0, 0))
    pl.semaphore_wait(barrier, len(peers) + nhead - 1)
    scatter(0)

    wide = jnp.concatenate([col] * (rows // HD), axis=1)
    t = lax.broadcasted_iota(jnp.int32, (rows, rows), 0)
    s = lax.broadcasted_iota(jnp.int32, (rows, rows), 1)
    visible = jnp.where((s <= t) & (wide == ids), 1.0, 0.0)
    loads[2].wait()
    for i in range(heads):
        hi, lo = split(dot(head(q_ref, i), head(k_ref, i), 1, 1) * visible)
        sc_hi[i], sc_lo[i] = hi, lo
        att[:, pl.ds(i * HD, HD)] = dot(hi, head(v_ref, i), 1, 0) + dot(lo, head(v_ref, i), 1, 0)
    loads[3].wait()
    wgt[...] = gain_ref[...] * g_ref[...].astype(F32)

    gather_wait(0)
    running(0, False)
    scatter(1)
    gather_wait(1)

    in_mask = (col == rcv[1, 0, pl.ds(piece, 1)]).astype(F32)
    square = jnp.zeros((rows, HD), F32)
    cross = jnp.zeros((rows, HD), F32)
    for i in range(heads):
        hi, lo = split(state(1, i))
        st_hi[i], st_lo[i] = hi, lo
        a = head(att, i) + in_mask * (dot(head(q_ref, i), hi, 1, 0) + dot(head(q_ref, i), lo, 1, 0))
        att[:, pl.ds(i * HD, HD)] = a
        square += a * a
        cross += a * head(wgt, i)
    ps_snd[0:1, :] = jnp.sum(square.T, axis=0, keepdims=True)
    ps_snd[1:2, :] = jnp.sum(cross.T, axis=0, keepdims=True)
    for d in range(1, nhead):
        pltpu.make_async_remote_copy(
            ps_snd, ps_rcv.at[h], ps_sem.at[0], ps_sem.at[1],
            device_id={"head": lax.rem(h + d, nhead)}, device_id_type=MESH,
        ).start()
    ps_rcv[h] = ps_snd[...]
    part = ps_rcv.at[pl.ds(0, nhead - 1)]
    pltpu.make_async_copy(part, part, ps_sem.at[1]).wait()
    sums = jnp.sum(ps_rcv[...], axis=0)
    inv = lax.rsqrt(sums[0:1] / features + EPSILON)
    back = inv * inv * sums[1:2] / features
    inv = jnp.broadcast_to(inv, (HD, rows)).T
    back = jnp.broadcast_to(back, (HD, rows)).T

    snd[2, :, pl.ds(piece, 1)] = jnp.broadcast_to(first[None], (nctx, 1, HD))
    first_mask = (col == first).astype(F32).astype(BF16)
    for i in range(heads):
        hi, lo = split(inv * (head(wgt, i) - head(att, i) * back))
        gr_hi[i], gr_lo[i] = hi, lo
        q = head(q_ref, i) * first_mask
        put_state(2, i, dot(q, hi, 0, 0) + dot(q, lo, 0, 0))
    scatter(2)

    def local_grads(i):
        ghi, glo = gr_hi[i], gr_lo[i]
        v = head(v_ref, i)
        bhi, blo = split((dot(ghi, v, 1, 1) + dot(glo, v, 1, 1)) * visible)
        shi, slo = st_hi[i], st_lo[i]
        gq = dot(bhi, head(k_ref, i), 1, 0) + dot(blo, head(k_ref, i), 1, 0)
        gq += in_mask * (dot(ghi, shi, 1, 1) + dot(ghi, slo, 1, 1) + dot(glo, shi, 1, 1))
        oq_ref[:, pl.ds(i * HD, HD)] = gq.astype(BF16)
        q = head(q_ref, i)
        lk[:, pl.ds(i * HD, HD)] = dot(bhi, q, 0, 0) + dot(blo, q, 0, 0)
        lv[:, pl.ds(i * HD, HD)] = dot(sc_hi[i], ghi, 0, 0) + dot(sc_hi[i], glo, 0, 0) + dot(sc_lo[i], ghi, 0, 0)

    for i in range(heads):
        local_grads(i)
    out_q = pltpu.make_async_copy(oq_ref, gq_hbm, out_sem.at[0])
    out_q.start()

    gather_wait(2)
    running(2, True)
    scatter(3)
    gather_wait(3)

    out_mask = (col == rcv[3, 0, pl.ds(piece, 1)]).astype(F32)
    for i in range(heads):
        hi, lo = split(state(3, i))
        v, k = head(v_ref, i), head(k_ref, i)
        ok_ref[:, pl.ds(i * HD, HD)] = (head(lk, i) + out_mask * (dot(v, hi, 1, 1) + dot(v, lo, 1, 1))).astype(BF16)
        ov_ref[:, pl.ds(i * HD, HD)] = (head(lv, i) + out_mask * (dot(k, hi, 1, 0) + dot(k, lo, 1, 0))).astype(BF16)
    out_k = pltpu.make_async_copy(ok_ref, gk_hbm, out_sem.at[1])
    out_v = pltpu.make_async_copy(ov_ref, gv_hbm, out_sem.at[2])
    out_k.start()
    out_v.start()

    for phase in range(4):
        part = snd.at[phase, pl.ds(0, nctx - 1), pl.ds(0, piece + 1)]
        pltpu.make_async_copy(part, part, send_sem.at[phase]).wait()
    part = ps_rcv.at[pl.ds(0, nhead - 1)]
    pltpu.make_async_copy(part, part, ps_sem.at[0]).wait()
    out_q.wait()
    out_k.wait()
    out_v.wait()


def solution(mesh):
    nctx, nhead = mesh.shape["ctx"], mesh.shape["head"]

    def on_device(queries, keys, values, out_grad, gain, segment_ids):
        rows, width = queries.shape
        heads = width // HD
        piece = width // nctx
        any_space = pl.BlockSpec(memory_space=pl.ANY)
        vmem = pl.BlockSpec(memory_space=pltpu.VMEM)
        wide = pltpu.VMEM((rows, width), BF16)
        total = pltpu.VMEM((rows, width), F32)
        return pl.pallas_call(
            functools.partial(kernel, nctx, nhead, width * nhead),
            out_shape=[jax.ShapeDtypeStruct((rows, width), BF16)] * 3,
            in_specs=[any_space] * 4 + [vmem] * 2,
            out_specs=[any_space] * 3,
            scratch_shapes=[wide] * 7
            + [
                pltpu.VMEM((4, nctx, piece + 8, HD), F32),
                pltpu.VMEM((4, nctx, piece + 8, HD), F32),
                pltpu.VMEM((2, rows), F32),
                pltpu.VMEM((nhead, 2, rows), F32),
                pltpu.VMEM((heads, rows, rows), BF16),
                pltpu.VMEM((heads, rows, rows), BF16),
                total,
                total,
                pltpu.VMEM((heads, rows, HD), BF16),
                pltpu.VMEM((heads, rows, HD), BF16),
                pltpu.VMEM((heads, HD, HD), BF16),
                pltpu.VMEM((heads, HD, HD), BF16),
                total,
                total,
                pltpu.SemaphoreType.DMA((4,)),
                pltpu.SemaphoreType.DMA((3,)),
                pltpu.SemaphoreType.DMA((4,)),
                pltpu.SemaphoreType.DMA((4,)),
                pltpu.SemaphoreType.DMA((2,)),
            ],
            compiler_params=pltpu.CompilerParams(
                collective_id=0, has_side_effects=True, vmem_limit_bytes=48 * 1024 * 1024
            ),
            name="scan_grads",
        )(queries, keys, values, out_grad, gain.reshape(1, width), segment_ids.reshape(1, rows))

    return jax.shard_map(
        on_device,
        mesh=mesh,
        in_specs=(
            P("ctx", "head"),
            P("ctx", "head"),
            P("ctx", "head"),
            P("ctx", "head"),
            P("head"),
            P("ctx"),
        ),
        out_specs=(P("ctx", "head"), P("ctx", "head"), P("ctx", "head")),
        check_vma=False,
    )
```

profile of v0, /device:TPU:1, one launch (start us, length us, event | category | flops | bytes accessed | tf_op | source)
XLA Modules:
  0.0 67.3 jit_solution(18070848404872586277)
XLA Ops:
  0.6 0.0 copy-start.4
  0.6 0.0 copy-start.5
  0.7 0.7 copy-done.4
  1.3 0.0 copy-done.5
  1.3 0.0 copy-start
  1.3 0.9 %copy-done = bf16[256,512]{1,0:T(8,128)(2,1)S(1)} copy-done((bf16[256,512]{1,0:T(8,128)(2,1)S(1)}, bf16[256,512]{1,0:T(8,128)(2,1)}, u32[]{:S(2)}) %copy-start) | copy-done | bytes 262168
  2.3 0.0 copy-start.1
  2.3 0.9 %copy-done.1 = bf16[256,512]{1,0:T(8,128)(2,1)S(1)} copy-done((bf16[256,512]{1,0:T(8,128)(2,1)S(1)}, bf16[256,512]{1,0:T(8,128)(2,1)}, u32[]{:S(2)}) %copy-start.1) | copy-done | bytes 262168
  3.2 0.0 copy-start.2
  3.2 0.9 %copy-done.2 = bf16[256,512]{1,0:T(8,128)(2,1)S(1)} copy-done((bf16[256,512]{1,0:T(8,128)(2,1)S(1)}, bf16[256,512]{1,0:T(8,128)(2,1)}, u32[]{:S(2)}) %copy-start.2) | copy-done | bytes 262168
  4.2 0.0 copy-start.3
  4.2 0.9 %copy-done.3 = bf16[256,512]{1,0:T(8,128)(2,1)S(1)} copy-done((bf16[256,512]{1,0:T(8,128)(2,1)S(1)}, bf16[256,512]{1,0:T(8,128)(2,1)}, u32[]{:S(2)}) %copy-start.3) | copy-done | bytes 262168
  5.1 60.1 %scan_grads.1 = (bf16[256,512]{1,0:T(8,128)(2,1)S(1)}, bf16[256,512]{1,0:T(8,128)(2,1)S(1)}, bf16[256,512]{1,0:T(8,128)(2,1)S(1)}) custom-call(bf16[256,512]{1,0:T(8,128)(2,1)S(1)} %copy-done, bf16[256,512]{1,0:T(8,128)(2,1)S(1)} %copy-done.1, bf16[256,512]{1,0:T(8,128)(2,1)S(1)} %copy-done.2, bf16[256,512]{1,0:T(8,128)(2,1)S(1)} %copy-done.3, ...), custom_call_target="tpu_custom_call" | custom-call | tf_op jit(solution)/shard_map/scan_grads/pallas_call | solution.py:216
  65.2 0.7 %copy.12 = bf16[256,512]{1,0:T(8,128)(2,1)} copy(bf16[256,512]{1,0:T(8,128)(2,1)S(1)} %get-tuple-element.6) | data formatting | bytes 524288
  65.9 0.7 %copy.13 = bf16[256,512]{1,0:T(8,128)(2,1)} copy(bf16[256,512]{1,0:T(8,128)(2,1)S(1)} %get-tuple-element.7) | data formatting | bytes 524288
  66.6 0.7 %copy.14 = bf16[256,512]{1,0:T(8,128)(2,1)} copy(bf16[256,512]{1,0:T(8,128)(2,1)S(1)} %get-tuple-element.8) | data formatting | bytes 524288
Async XLA Ops:
  0.6 0.7 %copy-start.4 = (f32[512]{0:T(512)S(1)}, f32[512]{0:T(512)}, u32[]{:S(2)}) copy-start(f32[512]{0:T(512)} %param.10) | copy-start | bytes 6148
  0.6 0.7 %copy-start.5 = (s32[256]{0:T(256)S(1)}, s32[256]{0:T(256)}, u32[]{:S(2)}) copy-start(s32[256]{0:T(256)} %param.11) | copy-start | bytes 3076
  1.3 0.9 %copy-start = (bf16[256,512]{1,0:T(8,128)(2,1)S(1)}, bf16[256,512]{1,0:T(8,128)(2,1)}, u32[]{:S(2)}) copy-start(bf16[256,512]{1,0:T(8,128)(2,1)} %q_hbm.1) | copy-start | bytes 786436
  2.3 0.9 %copy-start.1 = (bf16[256,512]{1,0:T(8,128)(2,1)S(1)}, bf16[256,512]{1,0:T(8,128)(2,1)}, u32[]{:S(2)}) copy-start(bf16[256,512]{1,0:T(8,128)(2,1)} %k_hbm.1) | copy-start | bytes 786436
  3.2 0.9 %copy-start.2 = (bf16[256,512]{1,0:T(8,128)(2,1)S(1)}, bf16[256,512]{1,0:T(8,128)(2,1)}, u32[]{:S(2)}) copy-start(bf16[256,512]{1,0:T(8,128)(2,1)} %v_hbm.1) | copy-start | bytes 786436
  4.2 0.9 %copy-start.3 = (bf16[256,512]{1,0:T(8,128)(2,1)S(1)}, bf16[256,512]{1,0:T(8,128)(2,1)}, u32[]{:S(2)}) copy-start(bf16[256,512]{1,0:T(8,128)(2,1)} %g_hbm.1) | copy-start | bytes 786436
where the time goes:
time: 67.6 us; the launch traced here: 67.3 us
  Pallas kernels  60.1 us (89%)
  local copies, waits for them, and re-layouts  6.59 us (10%)
    pallas_call x1, Pallas kernels, on_device(): pl.pallas_call(functools.partial(kernel, nctx, nhead, width * nhead), out...  60.1 us
    unnamed x15, local copies, waits for them, and re-layouts  6.59 us

commit v1 on v0

v1 whole, which is shorter than its diff:
```python
import functools
import random

import jax
import jax.numpy as jnp
from jax import lax
from jax.experimental import pallas as pl
from jax.experimental.pallas import tpu as pltpu
from jax.sharding import PartitionSpec as P

HD = 128
EPSILON = 1e-06
RING = 8
MESH = pl.DeviceIdType.MESH
F32 = jnp.float32
BF16 = jnp.bfloat16


def dot(a, b, ca, cb):
    return lax.dot_general(a, b, (((ca,), (cb,)), ((), ())), preferred_element_type=F32)


def split(x):
    hi = x.astype(BF16)
    return hi, (x - hi.astype(F32)).astype(BF16)


def parts(x, axis):
    return jnp.concatenate(split(x), axis=axis)


def twice(x):
    return jnp.concatenate([x, x], axis=1)


def kernel(
    nctx, nhead, features,
    q_hbm, k_hbm, v_hbm, g_hbm, gain_hbm, ids_hbm,
    oq_ref, ok_ref, ov_ref,
    q_ref, k_ref, v_ref, g_ref, gain_ref, ids_ref,
    snd, rcv, ps_snd, ps_rcv, keep_f, keep_b,
    vis_ref, sc_hi, sc_lo, att, wgt, gr, st, lk, lv, q_two, q_turn, k_two, v_two,
    in_sem, send_sem, recv_sem, ps_sem,
):
    rows, width = q_ref.shape
    heads = width // HD
    piece = snd.shape[2] - 8
    per = HD // piece
    nz = nctx // RING
    me = lax.axis_index("ctx")
    z, y = me // RING, me % RING
    h = lax.axis_index("head")
    turn = 1 - 2 * (h % 2)

    offsets = [(dz, dy) for dz in range(nz) for dy in range(RING) if dz or dy]
    random.Random(1).shuffle(offsets)
    offsets.sort(key=lambda o: -(min(o[0], nz - o[0]) + min(o[1], RING - o[1])))
    peers = [
        lax.rem(z + turn * dz + nz, nz) * RING + lax.rem(y + turn * dy + RING, RING) for dz, dy in offsets
    ]

    barrier = pltpu.get_barrier_semaphore()
    for p in peers:
        pl.semaphore_signal(barrier, inc=1, device_id={"ctx": p}, device_id_type=MESH)
    for d in range(1, nhead):
        pl.semaphore_signal(barrier, inc=1, device_id={"head": lax.rem(h + d, nhead)}, device_id_type=MESH)

    pairs = (
        (ids_hbm, ids_ref), (k_hbm, k_ref), (v_hbm, v_ref), (q_hbm, q_ref), (g_hbm, g_ref), (gain_hbm, gain_ref),
    )
    loads = [pltpu.make_async_copy(src, dst, in_sem.at[i]) for i, (src, dst) in enumerate(pairs)]
    for copy in loads:
        copy.start()

    def scatter(phase, size):
        for p in peers:
            pltpu.make_async_remote_copy(
                snd.at[phase, p, pl.ds(0, size)], rcv.at[phase, me, pl.ds(0, size)],
                send_sem.at[phase], recv_sem.at[phase],
                device_id={"ctx": p}, device_id_type=MESH,
            ).start()
        rcv[phase, me, pl.ds(0, size)] = snd[phase, me, pl.ds(0, size)]

    def gather_wait(phase, size):
        part = rcv.at[phase, pl.ds(0, nctx - 1), pl.ds(0, size)]
        pltpu.make_async_copy(part, part, recv_sem.at[phase]).wait()

    def running(phase, keep, backward):
        def step(i, total):
            e = nctx - 1 - i if backward else i
            snd[phase + 1, e, pl.ds(0, piece)] = total
            return rcv[phase, e, pl.ds(0, piece)] + jnp.where(keep[pl.ds(e, 1), :] > 0.0, total, 0.0)

        lax.fori_loop(0, nctx, step, jnp.zeros((piece, HD), F32), unroll=8)

    def state(phase, i):
        return rcv[phase, pl.ds(i * per, per), pl.ds(0, piece)].reshape(HD, HD)

    def put_state(phase, i, value):
        snd[phase, pl.ds(i * per, per), pl.ds(0, piece)] = value.reshape(per, piece, HD)

    def head(ref, i):
        return ref[:, pl.ds(i * HD, HD)]

    loads[0].wait()
    ids = ids_ref[...].astype(F32)
    col = jnp.broadcast_to(ids, (HD, rows)).T
    first, last = ids[:, 0:1], ids[:, rows - 1 : rows]
    lane = lax.broadcasted_iota(jnp.int32, (1, HD), 1)
    tags = jnp.where(lane < HD // 2, first, last)
    snd[0, :, pl.ds(piece, 1)] = jnp.broadcast_to(tags[None], (nctx, 1, HD))
    last_mask = (col == last).astype(F32).astype(BF16)
    loads[1].wait()
    loads[2].wait()
    for i in range(heads):
        put_state(0, i, dot(head(k_ref, i) * last_mask, head(v_ref, i), 0, 0))
    pl.semaphore_wait(barrier, len(peers) + nhead - 1)
    scatter(0, piece + 1)

    wide = jnp.concatenate([col] * (rows // HD), axis=1)
    t = lax.broadcasted_iota(jnp.int32, (rows, rows), 0)
    s = lax.broadcasted_iota(jnp.int32, (rows, rows), 1)
    vis_ref[...] = jnp.where((s <= t) & (wide == ids), 1.0, 0.0)
    first_mask = (col == first).astype(F32).astype(BF16)
    loads[3].wait()
    for i in range(heads):
        v = head(v_ref, i)
        hi, lo = split(dot(head(q_ref, i), head(k_ref, i), 1, 1) * vis_ref[...])
        sc_hi[i], sc_lo[i] = hi, lo
        att[:, pl.ds(i * HD, HD)] = dot(hi, v, 1, 0) + dot(lo, v, 1, 0)
        q_turn[i] = (head(q_ref, i) * first_mask).T
    loads[4].wait()
    loads[5].wait()
    wgt[...] = gain_ref[...] * g_ref[...].astype(F32)

    gather_wait(0, piece + 1)
    tags = rcv[0, :, pl.ds(piece, 1)].reshape(nctx, HD)
    firsts = jnp.broadcast_to(tags[:, 0:1], (nctx, HD))
    lasts = jnp.broadcast_to(tags[:, HD - 1 : HD], (nctx, HD))
    outside = jnp.full((1, HD), -1.0, F32)
    before = jnp.concatenate([outside, lasts[: nctx - 1]], axis=0)
    after = jnp.concatenate([firsts[1:], outside], axis=0)
    keep_f[...] = (lasts == before).astype(F32)
    running(0, keep_f, False)
    scatter(1, piece)

    keep_b[...] = (firsts == after).astype(F32)
    mine = lax.broadcasted_iota(jnp.int32, (nctx, HD), 0) == me
    tag_in = jnp.max(jnp.where(mine, before, -1.0), axis=0, keepdims=True)
    tag_out = jnp.max(jnp.where(mine, after, -1.0), axis=0, keepdims=True)
    in_mask = (col == tag_in).astype(F32)
    in_bf, out_bf = in_mask.astype(BF16), (col == tag_out).astype(F32).astype(BF16)
    for i in range(heads):
        q_two[i] = twice(head(q_ref, i) * in_bf)
        k_two[i] = twice(head(k_ref, i) * out_bf)
        v_two[i] = twice(head(v_ref, i) * out_bf)

    gather_wait(1, piece)
    square = jnp.zeros((rows, HD), F32)
    cross = jnp.zeros((rows, HD), F32)
    for i in range(heads):
        both = parts(state(1, i), 0)
        st[i] = both
        a = head(att, i) + dot(q_two[i], both, 1, 0)
        att[:, pl.ds(i * HD, HD)] = a
        square += a * a
        cross += a * head(wgt, i)
    ones = jnp.ones((16, 2 * HD), BF16)
    ps_snd[0:1, :] = dot(ones, parts(square, 1), 1, 1)[0:1]
    ps_snd[1:2, :] = dot(ones, parts(cross, 1), 1, 1)[0:1]
    for d in range(1, nhead):
        pltpu.make_async_remote_copy(
            ps_snd, ps_rcv.at[h], ps_sem.at[0], ps_sem.at[1],
            device_id={"head": lax.rem(h + d, nhead)}, device_id_type=MESH,
        ).start()
    ps_rcv[h] = ps_snd[...]
    part = ps_rcv.at[pl.ds(0, nhead - 1)]
    pltpu.make_async_copy(part, part, ps_sem.at[1]).wait()
    sums = jnp.sum(ps_rcv[...], axis=0)
    inv = lax.rsqrt(sums[0:1] / features + EPSILON)
    back = inv * inv * sums[1:2] / features

    def thirds(x):
        hi, rest = x.astype(BF16).astype(F32), x
        rest = rest - hi
        mid = rest.astype(BF16).astype(F32)
        return [hi, mid, rest - mid]

    table = jnp.concatenate(thirds(inv) + thirds(back) + [jnp.zeros((10, rows), F32)], axis=0).astype(BF16)
    r = lax.broadcasted_iota(jnp.int32, (16, 2 * HD), 0)
    c = lax.broadcasted_iota(jnp.int32, (16, 2 * HD), 1)
    pick = jnp.where((r < 3) == (c < HD), 1.0, 0.0).astype(BF16)
    columns = dot(table, pick, 0, 0)
    inv, back = columns[:, :HD], columns[:, HD:]

    for i in range(heads):
        both = parts(inv * (head(wgt, i) - head(att, i) * back), 1)
        gr[i] = both
        total = dot(q_turn[i], both, 1, 0)
        put_state(2, i, total[:, :HD] + total[:, HD:])
    scatter(2, piece)

    def local_grads(i):
        ghi, glo = gr[i, :, :HD], gr[i, :, HD:]
        v = head(v_ref, i)
        bhi, blo = split((dot(ghi, v, 1, 1) + dot(glo, v, 1, 1)) * vis_ref[...])
        shi, slo = st[i, :HD], st[i, HD:]
        gq = dot(ghi, shi, 1, 1) + dot(ghi, slo, 1, 1) + dot(glo, shi, 1, 1)
        gq = (col == tag_in).astype(F32) * gq + dot(bhi, head(k_ref, i), 1, 0) + dot(blo, head(k_ref, i), 1, 0)
        oq_ref[:, pl.ds(i * HD, HD)] = gq.astype(BF16)
        q = head(q_ref, i)
        lk[:, pl.ds(i * HD, HD)] = dot(bhi, q, 0, 0) + dot(blo, q, 0, 0)
        lv[:, pl.ds(i * HD, HD)] = dot(sc_hi[i], ghi, 0, 0) + dot(sc_hi[i], glo, 0, 0) + dot(sc_lo[i], ghi, 0, 0)

    for i in range(heads // 2):
        local_grads(i)

    gather_wait(2, piece)
    running(2, keep_b, True)
    scatter(3, piece)
    for i in range(heads // 2, heads):
        local_grads(i)
    gather_wait(3, piece)

    for i in range(heads):
        total = state(3, i)
        ok_ref[:, pl.ds(i * HD, HD)] = (head(lk, i) + dot(v_two[i], parts(total, 1), 1, 1)).astype(BF16)
        ov_ref[:, pl.ds(i * HD, HD)] = (head(lv, i) + dot(k_two[i], parts(total, 0), 1, 0)).astype(BF16)

    for phase, size in enumerate((piece + 1, piece, piece, piece)):
        part = snd.at[phase, pl.ds(0, nctx - 1), pl.ds(0, size)]
        pltpu.make_async_copy(part, part, send_sem.at[phase]).wait()
    part = ps_rcv.at[pl.ds(0, nhead - 1)]
    pltpu.make_async_copy(part, part, ps_sem.at[0]).wait()


def write_out(a_ref, b_ref, c_ref, a_hbm, b_hbm, c_hbm, sem):
    copies = [
        pltpu.make_async_copy(src, dst, sem.at[i])
        for i, (src, dst) in enumerate(((a_ref, a_hbm), (b_ref, b_hbm), (c_ref, c_hbm)))
    ]
    for copy in copies:
        copy.start()
    for copy in copies:
        copy.wait()


def solution(mesh):
    nctx, nhead = mesh.shape["ctx"], mesh.shape["head"]

    def on_device(queries, keys, values, out_grad, gain, segment_ids):
        rows, width = queries.shape
        heads = width // HD
        piece = width // nctx
        hbm = pl.BlockSpec(memory_space=pltpu.HBM)
        vmem = pl.BlockSpec(memory_space=pltpu.VMEM)
        wide = pltpu.VMEM((rows, width), BF16)
        total = pltpu.VMEM((rows, width), F32)
        double = pltpu.VMEM((heads, rows, 2 * HD), BF16)
        arrays = (queries, keys, values, out_grad, gain.reshape(1, width), segment_ids.reshape(1, rows))
        arrays = [pltpu.with_memory_space_constraint(x, pltpu.HBM) for x in arrays]
        grads = pl.pallas_call(
            functools.partial(kernel, nctx, nhead, width * nhead),
            out_shape=[pltpu.VMEM((rows, width), BF16)] * 3,
            in_specs=[hbm] * 6,
            out_specs=[vmem] * 3,
            scratch_shapes=[wide] * 4
            + [
                pltpu.VMEM((1, width), F32),
                pltpu.VMEM((1, rows), jnp.int32),
                pltpu.VMEM((4, nctx, piece + 8, HD), F32),
                pltpu.VMEM((4, nctx, piece + 8, HD), F32),
                pltpu.VMEM((2, rows), F32),
                pltpu.VMEM((nhead, 2, rows), F32),
                pltpu.VMEM((nctx, HD), F32),
                pltpu.VMEM((nctx, HD), F32),
                pltpu.VMEM((rows, rows), F32),
                pltpu.VMEM((heads, rows, rows), BF16),
                pltpu.VMEM((heads, rows, rows), BF16),
                total,
                total,
                double,
                pltpu.VMEM((heads, 2 * HD, HD), BF16),
                total,
                total,
                double,
                pltpu.VMEM((heads, HD, rows), BF16),
                double,
                double,
                pltpu.SemaphoreType.DMA((6,)),
                pltpu.SemaphoreType.DMA((4,)),
                pltpu.SemaphoreType.DMA((4,)),
                pltpu.SemaphoreType.DMA((2,)),
            ],
            compiler_params=pltpu.CompilerParams(
                collective_id=0, has_side_effects=True, vmem_limit_bytes=40 * 1024 * 1024
            ),
            name="scan_grads",
        )(*arrays)
        return pl.pallas_call(
            write_out,
            out_shape=[jax.ShapeDtypeStruct((rows, width), BF16)] * 3,
            in_specs=[pl.BlockSpec(memory_space=pl.ANY)] * 3,
            out_specs=[hbm] * 3,
            scratch_shapes=[pltpu.SemaphoreType.DMA((3,))],
            name="write_out",
        )(*[pltpu.with_memory_space_constraint(x, pltpu.VMEM) for x in grads])

    return jax.shard_map(
        on_device,
        mesh=mesh,
        in_specs=(
            P("ctx", "head"),
            P("ctx", "head"),
            P("ctx", "head"),
            P("ctx", "head"),
            P("head"),
            P("ctx"),
        ),
        out_specs=(P("ctx", "head"), P("ctx", "head"), P("ctx", "head")),
        check_vma=False,
    )
```

time: 67.6 us -> 60 us (0.89)
  local copies, waits for them, and re-layouts: 6.59 us -> 0 us
  Pallas kernels: 60.1 us -> 59.2 us
    unnamed x15 -> x0, local copies, waits for them, and re-layouts: 6.59 us -> none
    pallas_call x1, Pallas kernels: 60.1 us -> 58.3 us  [on_device(): pl.pallas_call(functools.partial(kernel, nctx, nhead, width * nhead), out...]
    pallas_call x0 -> x1, Pallas kernels: none -> 0.9 us  [on_device(): pl.pallas_call(write_out, out_shape=[jax.ShapeDtypeStruct((rows, width),...]
where the time goes in v1:
time: 60 us; the launch traced here: 59.9 us
  Pallas kernels  59.2 us (99%)
  between operations  0.64 us (1%)
    pallas_call x1, Pallas kernels, on_device(): pl.pallas_call(functools.partial(kernel, nctx, nhead, width * nhead), out...  58.3 us

profile of v1, /device:TPU:1, one launch (start us, length us, event | category | flops | bytes accessed | tf_op | source)
XLA Modules:
  0.0 59.9 jit_solution(4665940598960835251)
XLA Ops:
  0.6 58.3 %scan_grads.1 = (bf16[256,512]{1,0:T(8,128)(2,1)S(1)}, bf16[256,512]{1,0:T(8,128)(2,1)S(1)}, bf16[256,512]{1,0:T(8,128)(2,1)S(1)}) custom-call(bf16[256,512]{1,0:T(8,128)(2,1)} %q_hbm.1, bf16[256,512]{1,0:T(8,128)(2,1)} %k_hbm.1, bf16[256,512]{1,0:T(8,128)(2,1)} %v_hbm.1, bf16[256,512]{1,0:T(8,128)(2,1)} %g_hbm.1, f32[1,512]{1,0:T(1,128)} %bitcast.2, ...), custom_call_target="tpu_custom_call" | custom-call | tf_op jit(solution)/shard_map/scan_grads/pallas_call | solution.py:262
  59.0 0.9 %write_out.1 = (bf16[256,512]{1,0:T(8,128)(2,1)}, bf16[256,512]{1,0:T(8,128)(2,1)}, bf16[256,512]{1,0:T(8,128)(2,1)}) custom-call(bf16[256,512]{1,0:T(8,128)(2,1)S(1)} %get-tuple-element.6.a_ref, bf16[256,512]{1,0:T(8,128)(2,1)S(1)} %get-tuple-element.7.b_ref, bf16[256,512]{1,0:T(8,128)(2,1)S(1)} %get-tuple-element.8.c_ref), custom_call_target="tpu_custom_call" | custom-call | tf_op jit(solution)/shard_map/write_out/pallas_call | solution.py:300

commit v2 on v1

--- a/solution.py
+++ b/solution.py
@@ -11,6 +11,7 @@
 HD = 128
 EPSILON = 1e-06
 RING = 8
+EARLY = (0, 1, 7, 8, 2, 6)
 MESH = pl.DeviceIdType.MESH
 F32 = jnp.float32
 BF16 = jnp.bfloat16
@@ -40,7 +41,7 @@
     q_ref, k_ref, v_ref, g_ref, gain_ref, ids_ref,
     snd, rcv, ps_snd, ps_rcv, keep_f, keep_b,
     vis_ref, sc_hi, sc_lo, att, wgt, gr, st, lk, lv, q_two, q_turn, k_two, v_two,
-    in_sem, send_sem, recv_sem, ps_sem,
+    in_sem, send_sem, recv_sem, head_sem, ps_sem,
 ):
     rows, width = q_ref.shape
     heads = width // HD
@@ -53,7 +54,6 @@
     turn = 1 - 2 * (h % 2)
 
     offsets = [(dz, dy) for dz in range(nz) for dy in range(RING) if dz or dy]
-    random.Random(1).shuffle(offsets)
     offsets.sort(key=lambda o: -(min(o[0], nz - o[0]) + min(o[1], RING - o[1])))
     peers = [
         lax.rem(z + turn * dz + nz, nz) * RING + lax.rem(y + turn * dy + RING, RING) for dz, dy in offsets
@@ -72,18 +72,31 @@
     for copy in loads:
         copy.start()
 
-    def scatter(phase, size):
+    near = me // per
+
+    def send(phase, p, size, landed):
+        pltpu.make_async_remote_copy(
+            snd.at[phase, p, pl.ds(0, size)], rcv.at[phase, me, pl.ds(0, size)],
+            send_sem.at[phase], landed, device_id={"ctx": p}, device_id_type=MESH,
+        ).start()
+
+    def keep_own(phase, size, landed):
+        pltpu.make_async_copy(snd.at[phase, me, pl.ds(0, size)], rcv.at[phase, me, pl.ds(0, size)], landed).start()
+
+    def scatter(phase, size, landed):
         for p in peers:
-            pltpu.make_async_remote_copy(
-                snd.at[phase, p, pl.ds(0, size)], rcv.at[phase, me, pl.ds(0, size)],
-                send_sem.at[phase], recv_sem.at[phase],
-                device_id={"ctx": p}, device_id_type=MESH,
-            ).start()
-        rcv[phase, me, pl.ds(0, size)] = snd[phase, me, pl.ds(0, size)]
+            send(phase, p, size, landed)
+        keep_own(phase, size, landed)
 
     def gather_wait(phase, size):
-        part = rcv.at[phase, pl.ds(0, nctx - 1), pl.ds(0, size)]
+        part = rcv.at[phase, :, pl.ds(0, size)]
         pltpu.make_async_copy(part, part, recv_sem.at[phase]).wait()
+
+    def head_wait(phase, i):
+        part = rcv.at[phase, pl.ds(i * per, per), pl.ds(0, piece)]
+        pltpu.make_async_copy(part, part, head_sem.at[phase, i]).wait()
+
+    near_first = [lax.rem(near + d, heads) for d in sorted(range(heads), key=lambda d: min(d, heads - d))]
 
     def running(phase, keep, backward):
         def step(i, total):
@@ -115,7 +128,7 @@
     for i in range(heads):
         put_state(0, i, dot(head(k_ref, i) * last_mask, head(v_ref, i), 0, 0))
     pl.semaphore_wait(barrier, len(peers) + nhead - 1)
-    scatter(0, piece + 1)
+    scatter(0, piece + 1, recv_sem.at[0])
 
     wide = jnp.concatenate([col] * (rows // HD), axis=1)
     t = lax.broadcasted_iota(jnp.int32, (rows, rows), 0)
@@ -127,11 +140,12 @@
         v = head(v_ref, i)
         hi, lo = split(dot(head(q_ref, i), head(k_ref, i), 1, 1) * vis_ref[...])
         sc_hi[i], sc_lo[i] = hi, lo
-        att[:, pl.ds(i * HD, HD)] = dot(hi, v, 1, 0) + dot(lo, v, 1, 0)
+        att[i] = dot(hi, v, 1, 0) + dot(lo, v, 1, 0)
         q_turn[i] = (head(q_ref, i) * first_mask).T
     loads[4].wait()
     loads[5].wait()
-    wgt[...] = gain_ref[...] * g_ref[...].astype(F32)
+    for i in range(heads):
+        wgt[i] = head(gain_ref, i) * head(g_ref, i).astype(F32)
 
     gather_wait(0, piece + 1)
     tags = rcv[0, :, pl.ds(piece, 1)].reshape(nctx, HD)
@@ -142,7 +156,7 @@
     after = jnp.concatenate([firsts[1:], outside], axis=0)
     keep_f[...] = (lasts == before).astype(F32)
     running(0, keep_f, False)
-    scatter(1, piece)
+    scatter(1, piece, head_sem.at[1, near])
 
     keep_b[...] = (firsts == after).astype(F32)
     mine = lax.broadcasted_iota(jnp.int32, (nctx, HD), 0) == me
@@ -155,16 +169,16 @@
         k_two[i] = twice(head(k_ref, i) * out_bf)
         v_two[i] = twice(head(v_ref, i) * out_bf)
 
-    gather_wait(1, piece)
     square = jnp.zeros((rows, HD), F32)
     cross = jnp.zeros((rows, HD), F32)
-    for i in range(heads):
+    for i in near_first:
+        head_wait(1, i)
         both = parts(state(1, i), 0)
         st[i] = both
-        a = head(att, i) + dot(q_two[i], both, 1, 0)
-        att[:, pl.ds(i * HD, HD)] = a
+        a = att[i] + dot(q_two[i], both, 1, 0)
+        att[i] = a
         square += a * a
-        cross += a * head(wgt, i)
+        cross += a * wgt[i]
     ones = jnp.ones((16, 2 * HD), BF16)
     ps_snd[0:1, :] = dot(ones, parts(square, 1), 1, 1)[0:1]
     ps_snd[1:2, :] = dot(ones, parts(cross, 1), 1, 1)[0:1]
@@ -193,12 +207,12 @@
     columns = dot(table, pick, 0, 0)
     inv, back = columns[:, :HD], columns[:, HD:]
 
-    for i in range(heads):
-        both = parts(inv * (head(wgt, i) - head(att, i) * back), 1)
+    for i in reversed(near_first):
+        both = parts(inv * (wgt[i] - att[i] * back), 1)
         gr[i] = both
         total = dot(q_turn[i], both, 1, 0)
         put_state(2, i, total[:, :HD] + total[:, HD:])
-    scatter(2, piece)
+    scatter(2, piece, recv_sem.at[2])
 
     def local_grads(i):
         ghi, glo = gr[i, :, :HD], gr[i, :, HD:]
@@ -209,23 +223,28 @@
         gq = (col == tag_in).astype(F32) * gq + dot(bhi, head(k_ref, i), 1, 0) + dot(blo, head(k_ref, i), 1, 0)
         oq_ref[:, pl.ds(i * HD, HD)] = gq.astype(BF16)
         q = head(q_ref, i)
-        lk[:, pl.ds(i * HD, HD)] = dot(bhi, q, 0, 0) + dot(blo, q, 0, 0)
-        lv[:, pl.ds(i * HD, HD)] = dot(sc_hi[i], ghi, 0, 0) + dot(sc_hi[i], glo, 0, 0) + dot(sc_lo[i], ghi, 0, 0)
+        lk[i] = dot(bhi, q, 0, 0) + dot(blo, q, 0, 0)
+        lv[i] = dot(sc_hi[i], ghi, 0, 0) + dot(sc_hi[i], glo, 0, 0) + dot(sc_lo[i], ghi, 0, 0)
 
     for i in range(heads // 2):
         local_grads(i)
 
     gather_wait(2, piece)
     running(2, keep_b, True)
-    scatter(3, piece)
+    for p in EARLY:
+        pl.when(me != p)(functools.partial(send, 3, p, piece, head_sem.at[3, near]))
+    for p in peers:
+        others = functools.reduce(lambda a, b: a & b, [p != f for f in EARLY])
+        pl.when(others)(functools.partial(send, 3, p, piece, head_sem.at[3, near]))
+    keep_own(3, piece, head_sem.at[3, near])
     for i in range(heads // 2, heads):
         local_grads(i)
-    gather_wait(3, piece)
-
-    for i in range(heads):
+    for i in near_first:
+        head_wait(3, i)
         total = state(3, i)
-        ok_ref[:, pl.ds(i * HD, HD)] = (head(lk, i) + dot(v_two[i], parts(total, 1), 1, 1)).astype(BF16)
-        ov_ref[:, pl.ds(i * HD, HD)] = (head(lv, i) + dot(k_two[i], parts(total, 0), 1, 0)).astype(BF16)
+        at = pl.ds(pl.multiple_of(i * HD, HD), HD)
+        ok_ref[:, at] = (lk[i] + dot(v_two[i], parts(total, 1), 1, 1)).astype(BF16)
+        ov_ref[:, at] = (lv[i] + dot(k_two[i], parts(total, 0), 1, 0)).astype(BF16)
 
     for phase, size in enumerate((piece + 1, piece, piece, piece)):
         part = snd.at[phase, pl.ds(0, nctx - 1), pl.ds(0, size)]
@@ -255,7 +274,7 @@
         hbm = pl.BlockSpec(memory_space=pltpu.HBM)
         vmem = pl.BlockSpec(memory_space=pltpu.VMEM)
         wide = pltpu.VMEM((rows, width), BF16)
-        total = pltpu.VMEM((rows, width), F32)
+        total = pltpu.VMEM((heads, rows, HD), F32)
         double = pltpu.VMEM((heads, rows, 2 * HD), BF16)
         arrays = (queries, keys, values, out_grad, gain.reshape(1, width), segment_ids.reshape(1, rows))
         arrays = [pltpu.with_memory_space_constraint(x, pltpu.HBM) for x in arrays]
@@ -290,6 +309,7 @@
                 pltpu.SemaphoreType.DMA((6,)),
                 pltpu.SemaphoreType.DMA((4,)),
                 pltpu.SemaphoreType.DMA((4,)),
+                pltpu.SemaphoreType.DMA((4, heads)),
                 pltpu.SemaphoreType.DMA((2,)),
             ],
             compiler_params=pltpu.CompilerParams(

time: 60 us -> 59.4 us (0.990)
  Pallas kernels: 59.2 us -> 58.6 us
    pallas_call x1, Pallas kernels: 58.3 us -> 57.7 us  [on_device(): pl.pallas_call(functools.partial(kernel, nctx, nhead, width * nhead), out...]
where the time goes in v2:
time: 59.4 us; the launch traced here: 59.3 us
  Pallas kernels  58.6 us (99%)
  between operations  0.64 us (1%)
    pallas_call x1, Pallas kernels, on_device(): pl.pallas_call(functools.partial(kernel, nctx, nhead, width * nhead), out...  57.7 us

profile of v2, /device:TPU:1, one launch (start us, length us, event | category | flops | bytes accessed | tf_op | source)
XLA Modules:
  0.0 59.3 jit_solution(15615059384225986249)
XLA Ops:
  0.6 57.7 %scan_grads.1 = (bf16[256,512]{1,0:T(8,128)(2,1)S(1)}, bf16[256,512]{1,0:T(8,128)(2,1)S(1)}, bf16[256,512]{1,0:T(8,128)(2,1)S(1)}) custom-call(bf16[256,512]{1,0:T(8,128)(2,1)} %q_hbm.1, bf16[256,512]{1,0:T(8,128)(2,1)} %k_hbm.1, bf16[256,512]{1,0:T(8,128)(2,1)} %v_hbm.1, bf16[256,512]{1,0:T(8,128)(2,1)} %g_hbm.1, f32[1,512]{1,0:T(1,128)} %bitcast.2, ...), custom_call_target="tpu_custom_call" | custom-call | tf_op jit(solution)/shard_map/scan_grads/pallas_call | solution.py:281
  58.4 0.9 %write_out.1 = (bf16[256,512]{1,0:T(8,128)(2,1)}, bf16[256,512]{1,0:T(8,128)(2,1)}, bf16[256,512]{1,0:T(8,128)(2,1)}) custom-call(bf16[256,512]{1,0:T(8,128)(2,1)S(1)} %get-tuple-element.6.a_ref, bf16[256,512]{1,0:T(8,128)(2,1)S(1)} %get-tuple-element.7.b_ref, bf16[256,512]{1,0:T(8,128)(2,1)S(1)} %get-tuple-element.8.c_ref), custom_call_target="tpu_custom_call" | custom-call | tf_op jit(solution)/shard_map/write_out/pallas_call | solution.py:320

commit v3 on v2

--- a/solution.py
+++ b/solution.py
@@ -140,12 +140,12 @@
         v = head(v_ref, i)
         hi, lo = split(dot(head(q_ref, i), head(k_ref, i), 1, 1) * vis_ref[...])
         sc_hi[i], sc_lo[i] = hi, lo
-        att[i] = dot(hi, v, 1, 0) + dot(lo, v, 1, 0)
+        att[i] = (dot(hi, v, 1, 0) + dot(lo, v, 1, 0)).T
         q_turn[i] = (head(q_ref, i) * first_mask).T
     loads[4].wait()
     loads[5].wait()
     for i in range(heads):
-        wgt[i] = head(gain_ref, i) * head(g_ref, i).astype(F32)
+        wgt[i] = (head(gain_ref, i) * head(g_ref, i).astype(F32)).T
 
     gather_wait(0, piece + 1)
     tags = rcv[0, :, pl.ds(piece, 1)].reshape(nctx, HD)
@@ -169,19 +169,18 @@
         k_two[i] = twice(head(k_ref, i) * out_bf)
         v_two[i] = twice(head(v_ref, i) * out_bf)
 
-    square = jnp.zeros((rows, HD), F32)
-    cross = jnp.zeros((rows, HD), F32)
+    square = jnp.zeros((HD, rows), F32)
+    cross = jnp.zeros((HD, rows), F32)
     for i in near_first:
         head_wait(1, i)
-        both = parts(state(1, i), 0)
+        both = parts(state(1, i).T, 1)
         st[i] = both
-        a = att[i] + dot(q_two[i], both, 1, 0)
+        a = att[i] + dot(both, q_two[i], 1, 1)
         att[i] = a
         square += a * a
         cross += a * wgt[i]
-    ones = jnp.ones((16, 2 * HD), BF16)
-    ps_snd[0:1, :] = dot(ones, parts(square, 1), 1, 1)[0:1]
-    ps_snd[1:2, :] = dot(ones, parts(cross, 1), 1, 1)[0:1]
+    ps_snd[0:1, :] = jnp.sum(square, axis=0, keepdims=True)
+    ps_snd[1:2, :] = jnp.sum(cross, axis=0, keepdims=True)
     for d in range(1, nhead):
         pltpu.make_async_remote_copy(
             ps_snd, ps_rcv.at[h], ps_sem.at[0], ps_sem.at[1],
@@ -194,32 +193,27 @@
     inv = lax.rsqrt(sums[0:1] / features + EPSILON)
     back = inv * inv * sums[1:2] / features
 
-    def thirds(x):
-        hi, rest = x.astype(BF16).astype(F32), x
-        rest = rest - hi
-        mid = rest.astype(BF16).astype(F32)
-        return [hi, mid, rest - mid]
-
-    table = jnp.concatenate(thirds(inv) + thirds(back) + [jnp.zeros((10, rows), F32)], axis=0).astype(BF16)
-    r = lax.broadcasted_iota(jnp.int32, (16, 2 * HD), 0)
-    c = lax.broadcasted_iota(jnp.int32, (16, 2 * HD), 1)
-    pick = jnp.where((r < 3) == (c < HD), 1.0, 0.0).astype(BF16)
-    columns = dot(table, pick, 0, 0)
-    inv, back = columns[:, :HD], columns[:, HD:]
-
+    rows_of = per // RING
     for i in reversed(near_first):
-        both = parts(inv * (wgt[i] - att[i] * back), 1)
+        both = parts(inv * (wgt[i] - att[i] * back), 0)
         gr[i] = both
-        total = dot(q_turn[i], both, 1, 0)
+        total = dot(q_turn[i], both, 1, 1)
         put_state(2, i, total[:, :HD] + total[:, HD:])
-    scatter(2, piece, recv_sem.at[2])
+        for dy in sorted(range(RING), key=lambda d: -min(d, RING - d)):
+            py = lax.rem(y + turn * dy + RING, RING)
+            for r in range(rows_of):
+                p = (i * rows_of + lax.rem(z + r, rows_of)) * RING + py
+                if i is near_first[0] and dy == 0 and r == 0:
+                    keep_own(2, piece, recv_sem.at[2])
+                else:
+                    send(2, p, piece, recv_sem.at[2])
 
     def local_grads(i):
-        ghi, glo = gr[i, :, :HD], gr[i, :, HD:]
+        ghi, glo = gr[i, :HD].T, gr[i, HD:].T
         v = head(v_ref, i)
         bhi, blo = split((dot(ghi, v, 1, 1) + dot(glo, v, 1, 1)) * vis_ref[...])
-        shi, slo = st[i, :HD], st[i, HD:]
-        gq = dot(ghi, shi, 1, 1) + dot(ghi, slo, 1, 1) + dot(glo, shi, 1, 1)
+        shi, slo = st[i, :, :HD], st[i, :, HD:]
+        gq = dot(ghi, shi, 1, 0) + dot(ghi, slo, 1, 0) + dot(glo, shi, 1, 0)
         gq = (col == tag_in).astype(F32) * gq + dot(bhi, head(k_ref, i), 1, 0) + dot(blo, head(k_ref, i), 1, 0)
         oq_ref[:, pl.ds(i * HD, HD)] = gq.astype(BF16)
         q = head(q_ref, i)
@@ -275,6 +269,7 @@
         vmem = pl.BlockSpec(memory_space=pltpu.VMEM)
         wide = pltpu.VMEM((rows, width), BF16)
         total = pltpu.VMEM((heads, rows, HD), F32)
+        turned = pltpu.VMEM((heads, HD, rows), F32)
         double = pltpu.VMEM((heads, rows, 2 * HD), BF16)
         arrays = (queries, keys, values, out_grad, gain.reshape(1, width), segment_ids.reshape(1, rows))
         arrays = [pltpu.with_memory_space_constraint(x, pltpu.HBM) for x in arrays]
@@ -296,10 +291,10 @@
                 pltpu.VMEM((rows, rows), F32),
                 pltpu.VMEM((heads, rows, rows), BF16),
                 pltpu.VMEM((heads, rows, rows), BF16),
-                total,
-                total,
-                double,
-                pltpu.VMEM((heads, 2 * HD, HD), BF16),
+                turned,
+                turned,
+                pltpu.VMEM((heads, 2 * HD, rows), BF16),
+                pltpu.VMEM((heads, HD, 2 * HD), BF16),
                 total,
                 total,
                 double,

time: 59.4 us -> 58.7 us (0.988); the launches traced: 59.3 us -> 57.8 us
  Pallas kernels: 58.6 us -> 57.1 us
    pallas_call x1, Pallas kernels: 57.7 us -> 56.2 us  [on_device(): pl.pallas_call(functools.partial(kernel, nctx, nhead, width * nhead), out...]
where the time goes in v3:
time: 58.7 us; the launch traced here: 57.8 us
  Pallas kernels  57.1 us (97%)
  between operations  0.64 us (1%)
    pallas_call x1, Pallas kernels, on_device(): pl.pallas_call(functools.partial(kernel, nctx, nhead, width * nhead), out...  56.2 us

profile of v3, /device:TPU:1, one launch (start us, length us, event | category | flops | bytes accessed | tf_op | source)
XLA Modules:
  0.0 57.8 jit_solution(8625659388382963698)
XLA Ops:
  0.6 56.2 %scan_grads.1 = (bf16[256,512]{1,0:T(8,128)(2,1)S(1)}, bf16[256,512]{1,0:T(8,128)(2,1)S(1)}, bf16[256,512]{1,0:T(8,128)(2,1)S(1)}) custom-call(bf16[256,512]{1,0:T(8,128)(2,1)} %q_hbm.1, bf16[256,512]{1,0:T(8,128)(2,1)} %k_hbm.1, bf16[256,512]{1,0:T(8,128)(2,1)} %v_hbm.1, bf16[256,512]{1,0:T(8,128)(2,1)} %g_hbm.1, f32[1,512]{1,0:T(1,128)} %bitcast.2, ...), custom_call_target="tpu_custom_call" | custom-call | tf_op jit(solution)/shard_map/scan_grads/pallas_call | solution.py:276
  56.9 0.9 %write_out.1 = (bf16[256,512]{1,0:T(8,128)(2,1)}, bf16[256,512]{1,0:T(8,128)(2,1)}, bf16[256,512]{1,0:T(8,128)(2,1)}) custom-call(bf16[256,512]{1,0:T(8,128)(2,1)S(1)} %get-tuple-element.6.a_ref, bf16[256,512]{1,0:T(8,128)(2,1)S(1)} %get-tuple-element.7.b_ref, bf16[256,512]{1,0:T(8,128)(2,1)S(1)} %get-tuple-element.8.c_ref), custom_call_target="tpu_custom_call" | custom-call | tf_op jit(solution)/shard_map/write_out/pallas_call | solution.py:315

commit v4 on v3

--- a/solution.py
+++ b/solution.py
@@ -11,7 +11,7 @@
 HD = 128
 EPSILON = 1e-06
 RING = 8
-EARLY = (0, 1, 7, 8, 2, 6)
+EARLY = (1, 2, 9, 0, 8, 7, 10, 3)
 MESH = pl.DeviceIdType.MESH
 F32 = jnp.float32
 BF16 = jnp.bfloat16
@@ -181,7 +181,7 @@
         cross += a * wgt[i]
     ps_snd[0:1, :] = jnp.sum(square, axis=0, keepdims=True)
     ps_snd[1:2, :] = jnp.sum(cross, axis=0, keepdims=True)
-    for d in range(1, nhead):
+    for d in sorted(range(1, nhead), key=lambda d: -min(d, nhead - d)):
         pltpu.make_async_remote_copy(
             ps_snd, ps_rcv.at[h], ps_sem.at[0], ps_sem.at[1],
             device_id={"head": lax.rem(h + d, nhead)}, device_id_type=MESH,

time: 58.7 us -> 58.3 us (level)
  no operation moved by 1% of the time
where the time goes in v4:
time: 58.3 us; the launch traced here: 57.7 us
  Pallas kernels  57.1 us (98%)
  between operations  0.64 us (1%)
    pallas_call x1, Pallas kernels, on_device(): pl.pallas_call(functools.partial(kernel, nctx, nhead, width * nhead), out...  56.2 us

profile of v4, /device:TPU:1, one launch (start us, length us, event | category | flops | bytes accessed | tf_op | source)
XLA Modules:
  0.0 57.7 jit_solution(14913019958011943965)
XLA Ops:
  0.6 56.2 %scan_grads.1 = (bf16[256,512]{1,0:T(8,128)(2,1)S(1)}, bf16[256,512]{1,0:T(8,128)(2,1)S(1)}, bf16[256,512]{1,0:T(8,128)(2,1)S(1)}) custom-call(bf16[256,512]{1,0:T(8,128)(2,1)} %q_hbm.1, bf16[256,512]{1,0:T(8,128)(2,1)} %k_hbm.1, bf16[256,512]{1,0:T(8,128)(2,1)} %v_hbm.1, bf16[256,512]{1,0:T(8,128)(2,1)} %g_hbm.1, f32[1,512]{1,0:T(1,128)} %bitcast.2, ...), custom_call_target="tpu_custom_call" | custom-call | tf_op jit(solution)/shard_map/scan_grads/pallas_call | solution.py:276
  56.8 0.9 %write_out.1 = (bf16[256,512]{1,0:T(8,128)(2,1)}, bf16[256,512]{1,0:T(8,128)(2,1)}, bf16[256,512]{1,0:T(8,128)(2,1)}) custom-call(bf16[256,512]{1,0:T(8,128)(2,1)S(1)} %get-tuple-element.6.a_ref, bf16[256,512]{1,0:T(8,128)(2,1)S(1)} %get-tuple-element.7.b_ref, bf16[256,512]{1,0:T(8,128)(2,1)S(1)} %get-tuple-element.8.c_ref), custom_call_target="tpu_custom_call" | custom-call | tf_op jit(solution)/shard_map/write_out/pallas_call | solution.py:315
